TPU v7x, 32 devices: a whole 2x2x4 slice. The times are simulated.
32 devices in a mesh: lat: 8 (over z, x), deg: 4 (over y, core).
Axes of the slice: x: 2, y: 2, z: 4, core: 2. Of those that a mesh axis runs over, the one named last changes fastest.
Arguments:
- eta_tl: float32 [64, 10752], P('lat'), may hold values from -6 to 6
- vel_tl: float32 [2, 64, 10752], P(None, 'lat'), may hold values from -6 to 6
- eta_adj: float32 [64, 10752], P('lat'), may hold values from -6 to 6
- vel_adj: float32 [2, 64, 10752], P(None, 'lat'), may hold values from -6 to 6
- depth: float32 [64, 10752], P('lat'), may hold values from 0.2 to 1
- drag: float32 [64, 10752], P('lat'), may hold values from 0.01 to 0.3
- ocean: int32 [64, 10752], P('lat'), may hold values 0 or 1
- basis: bfloat16 [1024, 64, 1024], P('lat', None, 'deg'), may hold values from -5 to 5
- love: float32 [1024], P('deg'), may hold values from 0.05 to 0.5
Outputs:
- eta_tl_out: float32 [64, 10752], P('lat')
- vel_tl_out: float32 [2, 64, 10752], P(None, 'lat')
- eta_adj_out: float32 [64, 10752], P('lat')
- vel_adj_out: float32 [2, 64, 10752], P(None, 'lat')
All inputs are finite; a program needn't handle non-finite values. No bound on the sum of `ocean` on one device may be relied on, other than what follows from the above.
Results may differ from a plain program's by a relative error of at most 0.02.
Values may be sent and summed in bfloat16 or wider, within the bound.
A program may use at most 320 MiB of HBM per device.

v0:
```python
import jax
import jax.numpy as jnp
import numpy as np
from jax import lax
from jax.sharding import PartitionSpec as P

STEPS = 2
LANES = 128
kappa_x = 0.3
kappa_y = 0.4


def passed_along(value, axis, by):
    length = lax.axis_size(axis)
    pairs = [(i, i + by) for i in range(length) if 0 <= i + by < length]
    return lax.ppermute(value, axis, pairs)


def circle(numerator, period):
    angles = 2.0 * np.pi * (numerator % period) / period
    return (np.cos(angles), np.sin(angles))


def fourier_tables(lon_count, order_total):
    major = lon_count // LANES
    blocks = -(-order_total // major)
    residues, lanes = (np.arange(major), np.arange(LANES))
    outer = np.stack(circle(residues[:, None] * residues[None, :], major))
    turn = np.stack(circle(residues[:, None] * lanes[None, :], lon_count))
    inner = np.stack(circle(np.arange(blocks)[:, None] * lanes[None, :], LANES))
    return (
        jnp.asarray(outer, jnp.bfloat16),
        jnp.asarray(turn, jnp.float32),
        jnp.asarray(inner, jnp.bfloat16),
    )


def order_factor(orders):
    return jnp.where(orders == 0, 1.0, 2.0).astype(jnp.bfloat16)


def analyse(stacked, analysis_weight, tables, order_count):
    outer, turn, inner = tables
    row_count = stacked.shape[1]
    lon_count = stacked.shape[2]
    split_rows = stacked.astype(jnp.bfloat16).reshape(2 * row_count, lon_count // LANES, LANES)
    first = jnp.einsum("cka,rab->crkb", outer, split_rows, preferred_element_type=jnp.float32)
    turned = jnp.stack(
        [first[0] * turn[0] - first[1] * turn[1], first[1] * turn[0] + first[0] * turn[1]]
    ).astype(jnp.bfloat16)
    second = jnp.stack([jnp.stack([inner[0], -inner[1]]), jnp.stack([inner[1], inner[0]])])
    spectra = jnp.einsum("crkb,dcnb->dnkr", turned, second, preferred_element_type=jnp.float32)
    spectra = spectra.reshape(2, -1, 2, row_count)[:, :order_count] * (1.0 / lon_count)
    return (spectra * analysis_weight[None, None, :, :]).astype(jnp.bfloat16)


def legendre(spectra, basis, love):
    coeffs = jnp.einsum("cmfi,mil->cmfl", spectra, basis, preferred_element_type=jnp.float32)
    scaled = (coeffs * love[None, None, None, :]).astype(jnp.bfloat16)
    return jnp.einsum("cmfl,mil->cmfi", scaled, basis, preferred_element_type=jnp.float32)


def synthesise(coeffs, factors, tables, output_weight):
    outer, turn, inner = tables
    major, blocks = (turn.shape[1], inner.shape[1])
    order_count = coeffs.shape[1]
    row_count = coeffs.shape[3]
    scaled = coeffs * factors[None, :, None, None]
    padded = jnp.pad(scaled, ((0, 0), (0, major * blocks - order_count), (0, 0), (0, 0)))
    padded = padded.reshape(2, blocks, major, 2 * row_count)
    second = jnp.stack([jnp.stack([inner[0], inner[1]]), jnp.stack([-inner[1], inner[0]])])
    first = jnp.einsum("cnkr,dcnb->drkb", padded, second, preferred_element_type=jnp.float32)
    turned = jnp.stack(
        [first[0] * turn[0] + first[1] * turn[1], first[1] * turn[0] - first[0] * turn[1]]
    ).astype(jnp.bfloat16)
    grid_out = jnp.einsum("cka,crkb->rab", outer, turned, preferred_element_type=jnp.float32)
    return grid_out.reshape(2, row_count, -1) * output_weight[:, :, None]


def edges_from(rows, by):
    sent = jnp.concatenate(rows, 0).astype(jnp.bfloat16)
    got = passed_along(sent, "lat", by).astype(jnp.float32)
    return [got[i : i + 1] for i in range(len(rows))]


def northward(values, edge):
    return jnp.concatenate([values[1:], edge], 0)


def southward(values, edge):
    return jnp.concatenate([edge, values[:-1]], 0)


def on_device(eta_tl, vel_tl, eta_adj, vel_adj, depth, drag, ocean, basis, love):
    row_count = eta_tl.shape[0]
    lon_count = eta_tl.shape[1]
    lat_count = lax.axis_size("lat")
    total_rows = row_count * lat_count
    first_row = lax.axis_index("lat") * row_count
    indices = first_row + jnp.arange(row_count, dtype=jnp.int32)
    latitude = (indices.astype(jnp.float32) + 0.5) * (jnp.pi / total_rows) - 0.5 * jnp.pi
    cosine = jnp.cos(latitude)
    quad_weight = jnp.pi / total_rows * cosine
    east_factor = (kappa_x / (0.5 + 0.5 * cosine))[:, None]
    wet_mask = ocean.astype(jnp.float32)
    flux_north = kappa_y * wet_mask * eta_adj
    north_depth, north_wet, north_flux = edges_from([depth[:1], wet_mask[:1], flux_north[:1]], -1)
    depth_up = northward(depth, north_depth)
    wet_up = northward(wet_mask, north_wet)
    mask_u = wet_mask * jnp.roll(wet_mask, -1, 1)
    mask_v = wet_mask * wet_up
    depth_u = 0.5 * (depth + jnp.roll(depth, -1, 1))
    depth_v = 0.5 * (depth + depth_up)
    retain = 1.0 - drag
    ones_weight = jnp.ones_like(quad_weight)
    analysis_weight = jnp.stack([quad_weight, ones_weight])
    output_weight = jnp.stack([ones_weight, quad_weight])
    owned_count = basis.shape[0]
    order_total = owned_count * lat_count
    full_orders = jnp.arange(order_total, dtype=jnp.int32)
    tables = fourier_tables(lon_count, order_total)
    full_factor = order_factor(full_orders)
    state_eta, state_vel = (eta_tl, vel_tl)
    back_eta, back_vel = (eta_adj, vel_adj)

    def adjoint_terms(eta, vel, flux_edge):
        flux_east = east_factor * wet_mask * eta
        flux_up = kappa_y * wet_mask * eta
        north_up = northward(flux_up, flux_edge)
        p_term = mask_u * (vel[0] + depth_u * (jnp.roll(flux_east, -1, 1) - flux_east))
        q_term = mask_v * (vel[1] + depth_v * (north_up - flux_up))
        return (p_term, q_term)

    p_term, q_term = adjoint_terms(back_eta, back_vel, north_flux)
    (q_edge,) = edges_from([q_term[-1:]], 1)
    for step_index in range(STEPS):
        flux_p = east_factor * p_term
        q_down = southward(q_term, q_edge)
        psi_bar = flux_p - jnp.roll(flux_p, 1, 1) + kappa_y * (q_term - q_down)
        spectra = analyse(jnp.stack([state_eta, psi_bar]), analysis_weight, tables, order_total)
        owned_rows = lax.all_to_all(spectra, "lat", split_axis=1, concat_axis=3, tiled=True)
        partial_value = legendre(owned_rows, basis, love)
        total_sum = lax.psum(partial_value.astype(jnp.bfloat16), "deg")
        banded = lax.all_to_all(total_sum, "lat", split_axis=3, concat_axis=1, tiled=True)
        loads = synthesise(banded, full_factor, tables, output_weight)
        last = step_index == STEPS - 1
        psi_now = state_eta - loads[0]
        back_eta = back_eta + psi_bar - loads[1]
        back_vel = (retain * p_term, retain * q_term)
        north_rows = [psi_now[:1]]
        if not last:
            north_rows.append(kappa_y * wet_mask[:1] * back_eta[:1])
        north_edges = edges_from(north_rows, -1)
        psi_up = northward(psi_now, north_edges[0])
        new_u = mask_u * (
            retain * state_vel[0] - east_factor * (jnp.roll(psi_now, -1, 1) - psi_now)
        )
        new_v = mask_v * (retain * state_vel[1] - kappa_y * (psi_up - psi_now))
        flux_x = depth_u * new_u
        flux_y = depth_v * new_v
        south_rows = [flux_y[-1:]]
        if not last:
            p_term, q_term = adjoint_terms(back_eta, back_vel, north_edges[1])
            south_rows.append(q_term[-1:])
        south_edges = edges_from(south_rows, 1)
        flux_down = southward(flux_y, south_edges[0])
        if not last:
            q_edge = south_edges[1]
        state_eta = state_eta - wet_mask * (
            east_factor * (flux_x - jnp.roll(flux_x, 1, 1)) + kappa_y * (flux_y - flux_down)
        )
        state_vel = (new_u, new_v)
    state_vel, back_vel = (jnp.stack(state_vel), jnp.stack(back_vel))
    return (state_eta, state_vel, back_eta, back_vel)


def solution(mesh):
    in_specs = (
        P("lat", None),
        P(None, "lat", None),
        P("lat", None),
        P(None, "lat", None),
        P("lat", None),
        P("lat", None),
        P("lat", None),
        P("lat", None, "deg"),
        P("deg"),
    )
    out_specs = (P("lat", None), P(None, "lat", None), P("lat", None), P(None, "lat", None))
    return jax.shard_map(
        on_device, mesh=mesh, in_specs=in_specs, out_specs=out_specs, check_vma=False
    )
```

profile of v0, /device:TPU:0, one launch (start us, length us, event | category | flops | bytes accessed | tf_op | source)
XLA Modules:
  0.0 200.0 jit_solution(16623130963314955521)
XLA Ops:
  9.3 1.3 multiply_multiply_fusion.3
  13.4 4.8 %collective-permute-done = bf16[3,10752]{1,0:T(4,128)(2,1)S(1)} collective-permute-done((bf16[3,10752]{1,0:T(4,128)(2,1)S(1)}, bf16[3,10752]{1,0:T(4,128)(2,1)S(1)}, u32[]{:S(2)}, u32[]{:S(2)}) %collective-permute-start) | collective-permute-done | bytes 64544 | tf_op jit(solution)/shard_map/ppermute | solution.py:16
  19.7 4.8 %collective-permute-start.1 = (bf16[1,10752]{1,0:T(2,128)(2,1)S(1)}, bf16[1,10752]{1,0:T(2,128)(2,1)S(1)}, u32[]{:S(2)}, u32[]{:S(2)}) collective-permute-start(bf16[1,10752]{1,0:T(2,128)(2,1)S(1)} %slice.440), channel_id=1, source_target_pairs={{0,4},{4,8},{8,12},{12,16},{16,20},{20,24},{24,28},{1,5},{5,9},{9,... | collective-permute-start | bytes 64520 | tf_op jit(solution)/shard_map/ppermute | solution.py:16
  24.6 1.6 collective-permute-done.1
  31.1 12.4 %all_to_all.72 = bf16[8,2,2048]{2,1,0:T(2,128)(2,1)S(1)} all-to-all(bf16[8,2,2048]{2,1,0:T(2,128)(2,1)S(1)} %reshape.104), channel_id=1, replica_groups=mesh['lat'=8,'deg'=4] {'lat'}, dimensions={0} | all-to-all | bytes 131072 | tf_op jit(solution)/shard_map/all_to_all | solution.py:141
  44.7 1.3 copy.90
  46.2 6.0 %fusion.45 = bf16[2,128,2,64]{3,2,0,1:T(2,128)(2,1)} fusion(bf16[128,64,256]{2,1,0:T(8,128)(2,1)} %param.19, bf16[2,128,2,64]{3,2,0,1:T(2,128)(2,1)S(1)} %copy.60, f32[256]{0:T(256)S(1)} %copy-done.31), kind=kOutput, calls=%fused_computation.25 | convolution fusion | flops 33849344 | bytes 4326400 | tf_op jit(solution)/shard_map/cmfl,mil->cmfi/dot_general | solution.py:60
  52.2 29.1 %all-reduce.7.cloned.1.call-done = bf16[2,128,2,64]{3,2,0,1:T(2,128)(2,1)} async-done(((bf16[2,128,2,64]{3,2,0,1:T(2,128)(2,1)}), bf16[2,128,2,64]{3,2,0,1:T(2,128)(2,1)}) %all-reduce.7.cloned.1.call-update) | async-done | bytes 65552 | tf_op jit(solution)/shard_map/psum | solution.py:143
  81.3 1.7 copy.61
  83.0 5.5 %all-to-all-start.1 = ((bf16[2,128,2,64]{1,2,0,3:T(2,128)(2,1)}), bf16[2,128,2,64]{1,2,0,3:T(2,128)(2,1)S(1)}, u32[]{:S(2)}, u32[]{:S(2)}) async-start(bf16[2,128,2,64]{1,2,0,3:T(2,128)(2,1)} %copy.61), calls=%async_computation.1 | async-start | bytes 131072 | tf_op jit(solution)/shard_map/all_to_all | solution.py:144
  88.5 6.8 %all-to-all-done.1 = bf16[2,128,2,64]{1,2,0,3:T(2,128)(2,1)S(1)} async-done(((bf16[2,128,2,64]{1,2,0,3:T(2,128)(2,1)}), bf16[2,128,2,64]{1,2,0,3:T(2,128)(2,1)S(1)}, u32[]{:S(2)}, u32[]{:S(2)}) %all-to-all-start.1) | async-done | bytes 65568 | tf_op jit(solution)/shard_map/all_to_all | solution.py:144
  98.9 1.3 collective-permute-start.2
  101.4 3.5 %collective-permute-done.2 = bf16[2,10752]{1,0:T(2,128)(2,1)S(1)} collective-permute-done((bf16[2,10752]{1,0:T(2,128)(2,1)S(1)}, bf16[2,10752]{1,0:T(2,128)(2,1)S(1)}, u32[]{:S(2)}, u32[]{:S(2)}) %collective-permute-start.2) | collective-permute-done | bytes 43040 | tf_op jit(solution)/shard_map/ppermute | solution.py:16
  104.9 1.3 fusion.128
  106.5 3.4 %collective-permute-start.3 = (bf16[2,10752]{1,0:T(2,128)(2,1)S(1)}, bf16[2,10752]{1,0:T(2,128)(2,1)S(1)}, u32[]{:S(2)}, u32[]{:S(2)}) collective-permute-start(bf16[2,10752]{1,0:T(2,128)(2,1)S(1)} %pad_maximum_fusion.6), channel_id=1, source_target_pairs={{0,4},{4,8},{8,12},{12,16},{16,20},{20,24},{24,28},{1,5},{5,9},{9,... | collective-permute-start | bytes 129032 | tf_op jit(solution)/shard_map/ppermute | solution.py:16
  110.0 1.3 collective-permute-done.3
  115.8 10.6 %all_to_all.73 = bf16[8,2,2048]{2,1,0:T(2,128)(2,1)S(1)} all-to-all(bf16[8,2,2048]{2,1,0:T(2,128)(2,1)S(1)} %reshape.106), channel_id=1, replica_groups=mesh['lat'=8,'deg'=4] {'lat'}, dimensions={0} | all-to-all | bytes 131072 | tf_op jit(solution)/shard_map/all_to_all | solution.py:141
  127.6 1.3 copy.96
  129.1 6.0 %fusion.40 = bf16[2,128,2,64]{3,2,0,1:T(2,128)(2,1)} fusion(bf16[128,64,256]{2,1,0:T(8,128)(2,1)} %param.19, bf16[2,128,2,64]{3,2,0,1:T(2,128)(2,1)S(1)} %copy.69, f32[256]{0:T(256)S(1)} %copy-done.32), kind=kOutput, calls=%fused_computation.24 | convolution fusion | flops 33849344 | bytes 4326400 | tf_op jit(solution)/shard_map/cmfl,mil->cmfi/dot_general | solution.py:60
  135.1 28.1 %all-reduce.9.cloned.1.call-done = bf16[2,128,2,64]{3,2,0,1:T(2,128)(2,1)} async-done(((bf16[2,128,2,64]{3,2,0,1:T(2,128)(2,1)}), bf16[2,128,2,64]{3,2,0,1:T(2,128)(2,1)}) %all-reduce.9.cloned.1.call-update) | async-done | bytes 65552 | tf_op jit(solution)/shard_map/psum | solution.py:143
  164.3 12.2 %all_to_all.74 = bf16[2,128,2,64]{1,2,0,3:T(2,128)(2,1)S(1)} all-to-all(bf16[2,128,2,64]{1,2,0,3:T(2,128)(2,1)S(1)} %copy.70), channel_id=1, replica_groups=mesh['lat'=8,'deg'=4] {'lat'}, dimensions={3} | all-to-all | bytes 131072 | tf_op jit(solution)/shard_map/all_to_all | solution.py:144
  180.8 1.4 collective-permute-start.4
  183.3 3.5 %collective-permute-done.4 = bf16[1,10752]{1,0:T(2,128)(2,1)S(1)} collective-permute-done((bf16[1,10752]{1,0:T(2,128)(2,1)S(1)}, bf16[1,10752]{1,0:T(2,128)(2,1)S(1)}, u32[]{:S(2)}, u32[]{:S(2)}) %collective-permute-start.4) | collective-permute-done | bytes 21536 | tf_op jit(solution)/shard_map/ppermute | solution.py:16
  187.3 3.2 %collective-permute-start.5 = (bf16[1,10752]{1,0:T(2,128)(2,1)S(1)}, bf16[1,10752]{1,0:T(2,128)(2,1)S(1)}, u32[]{:S(2)}, u32[]{:S(2)}) collective-permute-start(bf16[1,10752]{1,0:T(2,128)(2,1)S(1)} %slice.435), channel_id=1, source_target_pairs={{0,4},{4,8},{8,12},{12,16},{16,20},{20,24},{24,28},{1,5},{5,9},{9,... | collective-permute-start | bytes 64520 | tf_op jit(solution)/shard_map/ppermute | solution.py:16
  (175 shorter events, 32.5 us)
Async XLA Ops:
  7.2 74.1 %all-reduce.7.cloned.1.call-start = ((), (), s32[]{:S(2)}) async-start(), calls=%async_computation.4 | async-start | bytes 262144 | tf_op jit(solution)/shard_map/psum | solution.py:143
  10.8 7.4 %collective-permute-start = (bf16[3,10752]{1,0:T(4,128)(2,1)S(1)}, bf16[3,10752]{1,0:T(4,128)(2,1)S(1)}, u32[]{:S(2)}, u32[]{:S(2)}) collective-permute-start(bf16[3,10752]{1,0:T(4,128)(2,1)S(1)} %pad_maximum_fusion.4), channel_id=1, source_target_pairs={{4,0},{8,4},{12,8},{16,12},{20,16},{24,20},{28,24},{5,1},{9,5},{13... | collective-permute-start | bytes 193544 | tf_op jit(solution)/shard_map/ppermute | solution.py:16
  12.5 5.8 %copy-start = (s32[8,10752]{1,0:T(8,128)S(1)}, s32[8,10752]{1,0:T(8,128)}, u32[]{:S(2)}) copy-start(s32[8,10752]{1,0:T(8,128)} %param.18) | copy-start | bytes 1032196
  12.5 5.8 %slice-start = ((f32[8,10752]{1,0:T(8,128)}), f32[8,1]{1,0:T(8,128)S(1)}, s32[]{:S(2)}) async-start(f32[8,10752]{1,0:T(8,128)} %copy-done.1), calls=%async_computation.6 | async-start | bytes 8192 | tf_op jit(solution)/shard_map/jit(_roll_static)/slice | solution.py:110
  12.5 5.8 %slice-start.1 = ((f32[8,10752]{1,0:T(8,128)}), f32[8,1]{1,0:T(8,128)S(1)}, s32[]{:S(2)}) async-start(f32[8,10752]{1,0:T(8,128)} %param.16), calls=%async_computation.7 | async-start | bytes 8192 | tf_op jit(solution)/shard_map/jit(_roll_static)/slice | solution.py:112
  12.6 5.8 %copy-start.23 = (f32[2,8,10752]{2,1,0:T(8,128)S(1)}, f32[2,8,10752]{2,1,0:T(8,128)}, u32[]{:S(2)}) copy-start(f32[2,8,10752]{2,1,0:T(8,128)} %param.15) | copy-start | bytes 2064388
  19.7 6.4 %collective-permute-start.1 = (bf16[1,10752]{1,0:T(2,128)(2,1)S(1)}, bf16[1,10752]{1,0:T(2,128)(2,1)S(1)}, u32[]{:S(2)}, u32[]{:S(2)}) collective-permute-start(bf16[1,10752]{1,0:T(2,128)(2,1)S(1)} %slice.440), channel_id=1, source_target_pairs={{0,4},{4,8},{8,12},{12,16},{16,20},{20,24},{24,28},{1,5},{5,9},{9,... | collective-permute-start | bytes 64520 | tf_op jit(solution)/shard_map/ppermute | solution.py:16
  24.5 72.2 %copy-start.27 = (f32[2,8]{1,0:T(2,128)}, f32[2,8]{1,0:T(2,128)S(1)}, u32[]{:S(2)}) copy-start(f32[2,8]{1,0:T(2,128)S(1)} %get-tuple-element.61) | copy-start | bytes 196
  31.1 15.1 %copy-start.31 = (f32[256]{0:T(256)S(1)}, f32[256]{0:T(256)}, u32[]{:S(2)}) copy-start(f32[256]{0:T(256)} %param.20) | copy-start | bytes 3076
  46.1 49.5 %copy-start.25 = (bf16[2,2,13,128,1]{3,2,1,0,4:T(8,128)(2,1)S(1)}, bf16[2,2,13,128,1]{3,2,1,0,4:T(8,128)(2,1)}, u32[]{:S(2)}) copy-start(bf16[2,2,13,128,1]{3,2,1,0,4:T(8,128)(2,1)} %constant.67) | copy-start | bytes 39940
  83.0 12.4 %all-to-all-start.1 = ((bf16[2,128,2,64]{1,2,0,3:T(2,128)(2,1)}), bf16[2,128,2,64]{1,2,0,3:T(2,128)(2,1)S(1)}, u32[]{:S(2)}, u32[]{:S(2)}) async-start(bf16[2,128,2,64]{1,2,0,3:T(2,128)(2,1)} %copy.61), calls=%async_computation.1 | async-start | bytes 131072 | tf_op jit(solution)/shard_map/all_to_all | solution.py:144
  88.5 74.7 %all-reduce.9.cloned.1.call-start = ((), (), s32[]{:S(2)}) async-start(), calls=%async_computation.5 | async-start | bytes 262144 | tf_op jit(solution)/shard_map/psum | solution.py:143
  98.9 5.9 %collective-permute-start.2 = (bf16[2,10752]{1,0:T(2,128)(2,1)S(1)}, bf16[2,10752]{1,0:T(2,128)(2,1)S(1)}, u32[]{:S(2)}, u32[]{:S(2)}) collective-permute-start(bf16[2,10752]{1,0:T(2,128)(2,1)S(1)} %pad_maximum_fusion.5), channel_id=1, source_target_pairs={{4,0},{8,4},{12,8},{16,12},{20,16},{24,20},{28,24},{5,1},{9,5},{13... | collective-permute-start | bytes 129032 | tf_op jit(solution)/shard_map/ppermute | solution.py:16
  106.5 4.9 %collective-permute-start.3 = (bf16[2,10752]{1,0:T(2,128)(2,1)S(1)}, bf16[2,10752]{1,0:T(2,128)(2,1)S(1)}, u32[]{:S(2)}, u32[]{:S(2)}) collective-permute-start(bf16[2,10752]{1,0:T(2,128)(2,1)S(1)} %pad_maximum_fusion.6), channel_id=1, source_target_pairs={{0,4},{4,8},{8,12},{12,16},{16,20},{20,24},{24,28},{1,5},{5,9},{9,... | collective-permute-start | bytes 129032 | tf_op jit(solution)/shard_map/ppermute | solution.py:16
  115.8 13.2 %copy-start.32 = (f32[256]{0:T(256)S(1)}, f32[256]{0:T(256)}, u32[]{:S(2)}) copy-start(f32[256]{0:T(256)} %param.20) | copy-start | bytes 3076
  129.0 47.7 %copy-start.26 = (bf16[2,2,13,128,1]{3,2,1,0,4:T(8,128)(2,1)S(1)}, bf16[2,2,13,128,1]{3,2,1,0,4:T(8,128)(2,1)}, u32[]{:S(2)}) copy-start(bf16[2,2,13,128,1]{3,2,1,0,4:T(8,128)(2,1)} %constant.67) | copy-start | bytes 39940
  135.1 42.1 %copy-start.22 = (f32[84,128]{1,0:T(8,128)S(1)}, f32[84,128]{1,0:T(8,128)}, u32[]{:S(2)}) copy-start(f32[84,128]{1,0:T(8,128)} %constant.64) | copy-start | bytes 129028
  180.7 6.2 %copy-start.6 = (f32[8,10752]{1,0:T(8,128)S(1)}, f32[8,10752]{1,0:T(8,128)}, u32[]{:S(2)}) copy-start(f32[8,10752]{1,0:T(8,128)} %param.17) | copy-start | bytes 1032196
  180.7 6.2 %copy-start.8 = (f32[8,10752]{1,0:T(8,128)S(1)}, f32[8,10752]{1,0:T(8,128)}, u32[]{:S(2)}) copy-start(f32[8,10752]{1,0:T(8,128)} %get-tuple-element.42) | copy-start | bytes 1032196
  180.7 6.2 %copy-start.10 = (f32[8,10752]{1,0:T(8,128)S(1)}, f32[8,10752]{1,0:T(8,128)}, u32[]{:S(2)}) copy-start(f32[8,10752]{1,0:T(8,128)} %get-tuple-element.43) | copy-start | bytes 1032196
  180.7 6.2 %copy-start.15 = (f32[8,10752]{1,0:T(8,128)S(1)}, f32[8,10752]{1,0:T(8,128)}, u32[]{:S(2)}) copy-start(f32[8,10752]{1,0:T(8,128)} %get-tuple-element.21) | copy-start | bytes 1032196
  180.7 6.2 %copy-start.16 = (f32[8,10752]{1,0:T(8,128)S(1)}, f32[8,10752]{1,0:T(8,128)}, u32[]{:S(2)}) copy-start(f32[8,10752]{1,0:T(8,128)} %get-tuple-element.40) | copy-start | bytes 1032196
  180.8 6.0 %collective-permute-start.4 = (bf16[1,10752]{1,0:T(2,128)(2,1)S(1)}, bf16[1,10752]{1,0:T(2,128)(2,1)S(1)}, u32[]{:S(2)}, u32[]{:S(2)}) collective-permute-start(bf16[1,10752]{1,0:T(2,128)(2,1)S(1)} %slice.436), channel_id=1, source_target_pairs={{4,0},{8,4},{12,8},{16,12},{20,16},{24,20},{28,24},{5,1},{9,5},{13... | collective-permute-start | bytes 64520 | tf_op jit(solution)/shard_map/ppermute | solution.py:16
  187.3 4.9 %collective-permute-start.5 = (bf16[1,10752]{1,0:T(2,128)(2,1)S(1)}, bf16[1,10752]{1,0:T(2,128)(2,1)S(1)}, u32[]{:S(2)}, u32[]{:S(2)}) collective-permute-start(bf16[1,10752]{1,0:T(2,128)(2,1)S(1)} %slice.435), channel_id=1, source_target_pairs={{0,4},{4,8},{8,12},{12,16},{16,20},{20,24},{24,28},{1,5},{5,9},{9,... | collective-permute-start | bytes 64520 | tf_op jit(solution)/shard_map/ppermute | solution.py:16
  (22 other events, 43.3 us)
Sparse Core Ops, SparseCore 0:
  52.3 28.9 all-reduce.6
  135.2 27.9 all-reduce.8
where the time goes:
time: 201 us; the launch traced here: 200 us
  waiting for transfers between devices  79.5 us (40%)
  blocking collectives  35.2 us (18%)
  starting transfers between devices  20.9 us (10%)
  local copies, waits for them, and re-layouts  20.4 us (10%)
  between operations  15 us (7%)
  matrix products  14.8 us (7%)
  other arithmetic  14.2 us (7%)
    psum x2, waiting for transfers between devices, on_device(): total_sum = lax.psum(partial_value.astype(jnp.bfloat16), 'deg')  57.2 us
    all_to_all x2, blocking collectives, on_device(): lax.all_to_all(spectra, 'lat', split_axis=1, concat_axis=3, tiled=True)  23 us
    ppermute x6, waiting for transfers between devices, passed_along(): return lax.ppermute(value, axis, pairs)  15.4 us
    ppermute x6, starting transfers between devices, passed_along(): return lax.ppermute(value, axis, pairs)  15.3 us
    all_to_all x1, blocking collectives, on_device(): lax.all_to_all(total_sum, 'lat', split_axis=3, concat_axis=1, tiled=True)  12.2 us
    dot_general x2, matrix products, legendre(): jnp.einsum('cmfl,mil->cmfi', scaled, basis, preferred_element_type=jnp.fl...  12 us
    unnamed x74, local copies, waits for them, and re-layouts  8.38 us
    all_to_all x1, waiting for transfers between devices, on_device(): lax.all_to_all(total_sum, 'lat', split_axis=3, concat_axis=1, tiled=True)  6.85 us
  transfers between devices with their start and end apart: 9, of which 9 were waited for; matrix products, arithmetic and copies ran while one was open for 2% of the time, Pallas kernels for 0%

commit v1 on v0

--- a/solution.py
+++ b/solution.py
@@ -140,7 +140,7 @@
         spectra = analyse(jnp.stack([state_eta, psi_bar]), analysis_weight, tables, order_total)
         owned_rows = lax.all_to_all(spectra, "lat", split_axis=1, concat_axis=3, tiled=True)
         partial_value = legendre(owned_rows, basis, love)
-        total_sum = lax.psum(partial_value.astype(jnp.bfloat16), "deg")
+        total_sum = jnp.sum(lax.all_gather(partial_value.astype(jnp.bfloat16), "deg"), axis=0)
         banded = lax.all_to_all(total_sum, "lat", split_axis=3, concat_axis=1, tiled=True)
         loads = synthesise(banded, full_factor, tables, output_weight)
         last = step_index == STEPS - 1

time: 201 us -> 139 us (0.69)
  waiting for transfers between devices: 79.5 us -> 22.3 us
  between operations: 15 us -> 1.57 us
  blocking collectives: 35.2 us -> 46.5 us
  other arithmetic: 14.2 us -> 16.5 us
  starting transfers between devices: 20.9 us -> 18.7 us
    psum x2 -> x0, waiting for transfers between devices: 57.2 us -> none  [on_device(): total_sum = lax.psum(partial_value.astype(jnp.bfloat16), 'deg')]
    all_gather x0 -> x2, blocking collectives: none -> 14.2 us  [on_device(): lax.all_gather(partial_value.astype(jnp.bfloat16), 'deg')]
    all_to_all x1, blocking collectives: 12.2 us -> 9.3 us  [on_device(): lax.all_to_all(total_sum, 'lat', split_axis=3, concat_axis=1, tiled=True)]
    psum x2 -> x0, local copies, waits for them, and re-layouts: 2.7 us -> none  [on_device(): total_sum = lax.psum(partial_value.astype(jnp.bfloat16), 'deg')]
    reduce_sum x0 -> x2, other arithmetic: none -> 2.33 us  [on_device(): jnp.sum(lax.all_gather(partial_value.astype(jnp.bfloat16), 'deg'), axis=0)]
    all_to_all x1, starting transfers between devices: 5.51 us -> 3.35 us  [on_device(): lax.all_to_all(total_sum, 'lat', split_axis=3, concat_axis=1, tiled=True)]
  transfers between devices with their start and end apart: 9 -> 7, of which waited for: 9 -> 7; matrix products, arithmetic and copies ran while one was open for 2% -> 3% of each run, Pallas kernels for 0% -> 0%
where the time goes in v1:
time: 139 us; the launch traced here: 138 us
  blocking collectives  46.5 us (33%)
  waiting for transfers between devices  22.3 us (16%)
  starting transfers between devices  18.7 us (13%)
  local copies, waits for them, and re-layouts  18.5 us (13%)
  other arithmetic  16.5 us (12%)
  matrix products  13.4 us (10%)
  between operations  1.57 us (1%)
    all_to_all x2, blocking collectives, on_device(): lax.all_to_all(spectra, 'lat', split_axis=1, concat_axis=3, tiled=True)  23 us
    ppermute x6, waiting for transfers between devices, passed_along(): return lax.ppermute(value, axis, pairs)  15.4 us
    ppermute x6, starting transfers between devices, passed_along(): return lax.ppermute(value, axis, pairs)  15.3 us
    all_gather x2, blocking collectives, on_device(): lax.all_gather(partial_value.astype(jnp.bfloat16), 'deg')  14.2 us
    dot_general x2, matrix products, legendre(): jnp.einsum('cmfl,mil->cmfi', scaled, basis, preferred_element_type=jnp.fl...  10.7 us
    all_to_all x1, blocking collectives, on_device(): lax.all_to_all(total_sum, 'lat', split_axis=3, concat_axis=1, tiled=True)  9.3 us
    unnamed x74, local copies, waits for them, and re-layouts  8.37 us
    all_to_all x1, waiting for transfers between devices, on_device(): lax.all_to_all(total_sum, 'lat', split_axis=3, concat_axis=1, tiled=True)  6.84 us
  transfers between devices with their start and end apart: 7, of which 7 were waited for; matrix products, arithmetic and copies ran while one was open for 3% of the time, Pallas kernels for 0%

profile of v1, /device:TPU:0, one launch (start us, length us, event | category | flops | bytes accessed | tf_op | source)
XLA Modules:
  0.0 137.5 jit_solution(17851817716444820063)
XLA Ops:
  2.8 1.3 multiply_multiply_fusion.3
  4.3 1.3 collective-permute-start
  6.8 4.8 %collective-permute-done = bf16[3,10752]{1,0:T(4,128)(2,1)S(1)} collective-permute-done((bf16[3,10752]{1,0:T(4,128)(2,1)S(1)}, bf16[3,10752]{1,0:T(4,128)(2,1)S(1)}, u32[]{:S(2)}, u32[]{:S(2)}) %collective-permute-start) | collective-permute-done | bytes 64544 | tf_op jit(solution)/shard_map/ppermute | solution.py:16
  13.1 4.8 %collective-permute-start.1 = (bf16[1,10752]{1,0:T(2,128)(2,1)S(1)}, bf16[1,10752]{1,0:T(2,128)(2,1)S(1)}, u32[]{:S(2)}, u32[]{:S(2)}) collective-permute-start(bf16[1,10752]{1,0:T(2,128)(2,1)S(1)} %slice.440), channel_id=1, source_target_pairs={{0,4},{4,8},{8,12},{12,16},{16,20},{20,24},{24,28},{1,5},{5,9},{9,... | collective-permute-start | bytes 64520 | tf_op jit(solution)/shard_map/ppermute | solution.py:16
  18.0 1.6 %collective-permute-done.1 = bf16[1,10752]{1,0:T(2,128)(2,1)S(1)} collective-permute-done((bf16[1,10752]{1,0:T(2,128)(2,1)S(1)}, bf16[1,10752]{1,0:T(2,128)(2,1)S(1)}, u32[]{:S(2)}, u32[]{:S(2)}) %collective-permute-start.1) | collective-permute-done | bytes 21536 | tf_op jit(solution)/shard_map/ppermute | solution.py:16
  24.5 12.4 %all_to_all.72 = bf16[8,2,2048]{2,1,0:T(2,128)(2,1)S(1)} all-to-all(bf16[8,2,2048]{2,1,0:T(2,128)(2,1)S(1)} %reshape.106), channel_id=1, replica_groups=mesh['lat'=8,'deg'=4] {'lat'}, dimensions={0} | all-to-all | bytes 131072 | tf_op jit(solution)/shard_map/all_to_all | solution.py:141
  38.1 1.3 copy.87
  39.6 5.3 %fusion.45 = bf16[2,128,2,64]{3,2,0,1:T(2,128)(2,1)S(1)} fusion(bf16[128,64,256]{2,1,0:T(8,128)(2,1)} %param.19, bf16[2,128,2,64]{3,2,0,1:T(2,128)(2,1)S(1)} %copy.57, f32[256]{0:T(256)S(1)} %copy-done.31), kind=kOutput, calls=%fused_computation.25 | convolution fusion | flops 33849344 | bytes 4326400 | tf_op jit(solution)/shard_map/cmfl,mil->cmfi/dot_general | solution.py:60
  44.9 7.5 %all-gather = bf16[8,128,2,64]{3,2,0,1:T(2,128)(2,1)S(1)} all-gather(bf16[2,128,2,64]{3,2,0,1:T(2,128)(2,1)S(1)} %fusion.45), channel_id=2, replica_groups=mesh['lat'=8,'deg'=4] {'deg'}, dimensions={0}, use_global_device_ids=true | all-gather | bytes 327680 | tf_op jit(solution)/shard_map/all_gather | solution.py:143
  54.3 3.3 %all-to-all-start.1 = ((bf16[2,128,2,64]{1,2,0,3:T(2,128)(2,1)}), bf16[2,128,2,64]{1,2,0,3:T(2,128)(2,1)S(1)}, u32[]{:S(2)}, u32[]{:S(2)}) async-start(bf16[2,128,2,64]{1,2,0,3:T(2,128)(2,1)} %copy.58), calls=%async_computation.1 | async-start | bytes 131072 | tf_op jit(solution)/shard_map/all_to_all | solution.py:144
  57.6 6.8 %all-to-all-done.1 = bf16[2,128,2,64]{1,2,0,3:T(2,128)(2,1)S(1)} async-done(((bf16[2,128,2,64]{1,2,0,3:T(2,128)(2,1)}), bf16[2,128,2,64]{1,2,0,3:T(2,128)(2,1)S(1)}, u32[]{:S(2)}, u32[]{:S(2)}) %all-to-all-start.1) | async-done | bytes 65568 | tf_op jit(solution)/shard_map/all_to_all | solution.py:144
  68.0 1.3 collective-permute-start.2
  70.5 3.5 %collective-permute-done.2 = bf16[2,10752]{1,0:T(2,128)(2,1)S(1)} collective-permute-done((bf16[2,10752]{1,0:T(2,128)(2,1)S(1)}, bf16[2,10752]{1,0:T(2,128)(2,1)S(1)}, u32[]{:S(2)}, u32[]{:S(2)}) %collective-permute-start.2) | collective-permute-done | bytes 43040 | tf_op jit(solution)/shard_map/ppermute | solution.py:16
  74.0 1.3 fusion.128
  75.6 3.4 %collective-permute-start.3 = (bf16[2,10752]{1,0:T(2,128)(2,1)S(1)}, bf16[2,10752]{1,0:T(2,128)(2,1)S(1)}, u32[]{:S(2)}, u32[]{:S(2)}) collective-permute-start(bf16[2,10752]{1,0:T(2,128)(2,1)S(1)} %pad_maximum_fusion.6), channel_id=1, source_target_pairs={{0,4},{4,8},{8,12},{12,16},{16,20},{20,24},{24,28},{1,5},{5,9},{9,... | collective-permute-start | bytes 129032 | tf_op jit(solution)/shard_map/ppermute | solution.py:16
  79.1 1.3 collective-permute-done.3
  84.9 10.6 %all_to_all.73 = bf16[8,2,2048]{2,1,0:T(2,128)(2,1)S(1)} all-to-all(bf16[8,2,2048]{2,1,0:T(2,128)(2,1)S(1)} %reshape.108), channel_id=1, replica_groups=mesh['lat'=8,'deg'=4] {'lat'}, dimensions={0} | all-to-all | bytes 131072 | tf_op jit(solution)/shard_map/all_to_all | solution.py:141
  96.7 1.3 copy.93
  98.2 5.3 %fusion.40 = bf16[2,128,2,64]{3,2,0,1:T(2,128)(2,1)S(1)} fusion(bf16[128,64,256]{2,1,0:T(8,128)(2,1)} %param.19, bf16[2,128,2,64]{3,2,0,1:T(2,128)(2,1)S(1)} %copy.66, f32[256]{0:T(256)S(1)} %copy-done.32), kind=kOutput, calls=%fused_computation.24 | convolution fusion | flops 33849344 | bytes 4326400 | tf_op jit(solution)/shard_map/cmfl,mil->cmfi/dot_general | solution.py:60
  103.5 6.8 %all-gather.1 = bf16[8,128,2,64]{3,2,0,1:T(2,128)(2,1)S(1)} all-gather(bf16[2,128,2,64]{3,2,0,1:T(2,128)(2,1)S(1)} %fusion.40), channel_id=3, replica_groups=mesh['lat'=8,'deg'=4] {'deg'}, dimensions={0}, use_global_device_ids=true | all-gather | bytes 327680 | tf_op jit(solution)/shard_map/all_gather | solution.py:143
  111.5 9.3 %all_to_all.74 = bf16[2,128,2,64]{1,2,0,3:T(2,128)(2,1)S(1)} all-to-all(bf16[2,128,2,64]{1,2,0,3:T(2,128)(2,1)S(1)} %copy.67), channel_id=1, replica_groups=mesh['lat'=8,'deg'=4] {'lat'}, dimensions={3} | all-to-all | bytes 131072 | tf_op jit(solution)/shard_map/all_to_all | solution.py:144
  125.1 1.4 %collective-permute-start.4 = (bf16[1,10752]{1,0:T(2,128)(2,1)S(1)}, bf16[1,10752]{1,0:T(2,128)(2,1)S(1)}, u32[]{:S(2)}, u32[]{:S(2)}) collective-permute-start(bf16[1,10752]{1,0:T(2,128)(2,1)S(1)} %slice.436), channel_id=1, source_target_pairs={{4,0},{8,4},{12,8},{16,12},{20,16},{24,20},{28,24},{5,1},{9,5},{13... | collective-permute-start | bytes 64520 | tf_op jit(solution)/shard_map/ppermute | solution.py:16
  127.7 3.5 %collective-permute-done.4 = bf16[1,10752]{1,0:T(2,128)(2,1)S(1)} collective-permute-done((bf16[1,10752]{1,0:T(2,128)(2,1)S(1)}, bf16[1,10752]{1,0:T(2,128)(2,1)S(1)}, u32[]{:S(2)}, u32[]{:S(2)}) %collective-permute-start.4) | collective-permute-done | bytes 21536 | tf_op jit(solution)/shard_map/ppermute | solution.py:16
  131.6 3.2 %collective-permute-start.5 = (bf16[1,10752]{1,0:T(2,128)(2,1)S(1)}, bf16[1,10752]{1,0:T(2,128)(2,1)S(1)}, u32[]{:S(2)}, u32[]{:S(2)}) collective-permute-start(bf16[1,10752]{1,0:T(2,128)(2,1)S(1)} %slice.435), channel_id=1, source_target_pairs={{0,4},{4,8},{8,12},{12,16},{16,20},{20,24},{24,28},{1,5},{5,9},{9,... | collective-permute-start | bytes 64520 | tf_op jit(solution)/shard_map/ppermute | solution.py:16
  (173 shorter events, 33.3 us)
Async XLA Ops:
  4.3 7.4 %collective-permute-start = (bf16[3,10752]{1,0:T(4,128)(2,1)S(1)}, bf16[3,10752]{1,0:T(4,128)(2,1)S(1)}, u32[]{:S(2)}, u32[]{:S(2)}) collective-permute-start(bf16[3,10752]{1,0:T(4,128)(2,1)S(1)} %pad_maximum_fusion.4), channel_id=1, source_target_pairs={{4,0},{8,4},{12,8},{16,12},{20,16},{24,20},{28,24},{5,1},{9,5},{13... | collective-permute-start | bytes 193544 | tf_op jit(solution)/shard_map/ppermute | solution.py:16
  5.9 5.8 %copy-start = (s32[8,10752]{1,0:T(8,128)S(1)}, s32[8,10752]{1,0:T(8,128)}, u32[]{:S(2)}) copy-start(s32[8,10752]{1,0:T(8,128)} %param.18) | copy-start | bytes 1032196
  6.0 5.8 %slice-start = ((f32[8,10752]{1,0:T(8,128)}), f32[8,1]{1,0:T(8,128)S(1)}, s32[]{:S(2)}) async-start(f32[8,10752]{1,0:T(8,128)} %copy-done.1), calls=%async_computation.4 | async-start | bytes 8192 | tf_op jit(solution)/shard_map/jit(_roll_static)/slice | solution.py:110
  6.0 5.8 %slice-start.1 = ((f32[8,10752]{1,0:T(8,128)}), f32[8,1]{1,0:T(8,128)S(1)}, s32[]{:S(2)}) async-start(f32[8,10752]{1,0:T(8,128)} %param.16), calls=%async_computation.5 | async-start | bytes 8192 | tf_op jit(solution)/shard_map/jit(_roll_static)/slice | solution.py:112
  6.0 5.8 %copy-start.23 = (f32[2,8,10752]{2,1,0:T(8,128)S(1)}, f32[2,8,10752]{2,1,0:T(8,128)}, u32[]{:S(2)}) copy-start(f32[2,8,10752]{2,1,0:T(8,128)} %param.15) | copy-start | bytes 2064388
  13.1 6.4 %collective-permute-start.1 = (bf16[1,10752]{1,0:T(2,128)(2,1)S(1)}, bf16[1,10752]{1,0:T(2,128)(2,1)S(1)}, u32[]{:S(2)}, u32[]{:S(2)}) collective-permute-start(bf16[1,10752]{1,0:T(2,128)(2,1)S(1)} %slice.440), channel_id=1, source_target_pairs={{0,4},{4,8},{8,12},{12,16},{16,20},{20,24},{24,28},{1,5},{5,9},{9,... | collective-permute-start | bytes 64520 | tf_op jit(solution)/shard_map/ppermute | solution.py:16
  17.9 4.7 %copy-start.29 = (f32[2,8]{1,0:T(2,128)}, f32[2,8]{1,0:T(2,128)S(1)}, u32[]{:S(2)}) copy-start(f32[2,8]{1,0:T(2,128)S(1)} %get-tuple-element.62) | copy-start | bytes 196
  17.9 47.9 %copy-start.27 = (f32[2,8]{1,0:T(2,128)}, f32[2,8]{1,0:T(2,128)S(1)}, u32[]{:S(2)}) copy-start(f32[2,8]{1,0:T(2,128)S(1)} %get-tuple-element.61) | copy-start | bytes 196
  24.5 15.1 %copy-start.31 = (f32[256]{0:T(256)S(1)}, f32[256]{0:T(256)}, u32[]{:S(2)}) copy-start(f32[256]{0:T(256)} %param.20) | copy-start | bytes 3076
  44.9 19.8 %copy-start.25 = (bf16[2,2,13,128,1]{3,2,1,0,4:T(8,128)(2,1)S(1)}, bf16[2,2,13,128,1]{3,2,1,0,4:T(8,128)(2,1)}, u32[]{:S(2)}) copy-start(bf16[2,2,13,128,1]{3,2,1,0,4:T(8,128)(2,1)} %constant.70) | copy-start | bytes 39940
  54.3 10.2 %all-to-all-start.1 = ((bf16[2,128,2,64]{1,2,0,3:T(2,128)(2,1)}), bf16[2,128,2,64]{1,2,0,3:T(2,128)(2,1)S(1)}, u32[]{:S(2)}, u32[]{:S(2)}) async-start(bf16[2,128,2,64]{1,2,0,3:T(2,128)(2,1)} %copy.58), calls=%async_computation.1 | async-start | bytes 131072 | tf_op jit(solution)/shard_map/all_to_all | solution.py:144
  68.0 5.9 %collective-permute-start.2 = (bf16[2,10752]{1,0:T(2,128)(2,1)S(1)}, bf16[2,10752]{1,0:T(2,128)(2,1)S(1)}, u32[]{:S(2)}, u32[]{:S(2)}) collective-permute-start(bf16[2,10752]{1,0:T(2,128)(2,1)S(1)} %pad_maximum_fusion.5), channel_id=1, source_target_pairs={{4,0},{8,4},{12,8},{16,12},{20,16},{24,20},{28,24},{5,1},{9,5},{13... | collective-permute-start | bytes 129032 | tf_op jit(solution)/shard_map/ppermute | solution.py:16
  70.2 3.8 %copy-start.24 = (f32[2,8,10752]{2,1,0:T(8,128)S(1)}, f32[2,8,10752]{2,1,0:T(8,128)}, u32[]{:S(2)}) copy-start(f32[2,8,10752]{2,1,0:T(8,128)} %param.13) | copy-start | bytes 2064388
  75.6 4.9 %collective-permute-start.3 = (bf16[2,10752]{1,0:T(2,128)(2,1)S(1)}, bf16[2,10752]{1,0:T(2,128)(2,1)S(1)}, u32[]{:S(2)}, u32[]{:S(2)}) collective-permute-start(bf16[2,10752]{1,0:T(2,128)(2,1)S(1)} %pad_maximum_fusion.6), channel_id=1, source_target_pairs={{0,4},{4,8},{8,12},{12,16},{16,20},{20,24},{24,28},{1,5},{5,9},{9,... | collective-permute-start | bytes 129032 | tf_op jit(solution)/shard_map/ppermute | solution.py:16
  84.9 13.2 %copy-start.32 = (f32[256]{0:T(256)S(1)}, f32[256]{0:T(256)}, u32[]{:S(2)}) copy-start(f32[256]{0:T(256)} %param.20) | copy-start | bytes 3076
  103.5 17.6 %copy-start.26 = (bf16[2,2,13,128,1]{3,2,1,0,4:T(8,128)(2,1)S(1)}, bf16[2,2,13,128,1]{3,2,1,0,4:T(8,128)(2,1)}, u32[]{:S(2)}) copy-start(bf16[2,2,13,128,1]{3,2,1,0,4:T(8,128)(2,1)} %constant.70) | copy-start | bytes 39940
  110.3 11.2 %copy-start.22 = (f32[84,128]{1,0:T(8,128)S(1)}, f32[84,128]{1,0:T(8,128)}, u32[]{:S(2)}) copy-start(f32[84,128]{1,0:T(8,128)} %constant.67) | copy-start | bytes 129028
  125.1 6.2 %copy-start.6 = (f32[8,10752]{1,0:T(8,128)S(1)}, f32[8,10752]{1,0:T(8,128)}, u32[]{:S(2)}) copy-start(f32[8,10752]{1,0:T(8,128)} %param.17) | copy-start | bytes 1032196
  125.1 6.2 %copy-start.8 = (f32[8,10752]{1,0:T(8,128)S(1)}, f32[8,10752]{1,0:T(8,128)}, u32[]{:S(2)}) copy-start(f32[8,10752]{1,0:T(8,128)} %get-tuple-element.42) | copy-start | bytes 1032196
  125.1 6.2 %copy-start.10 = (f32[8,10752]{1,0:T(8,128)S(1)}, f32[8,10752]{1,0:T(8,128)}, u32[]{:S(2)}) copy-start(f32[8,10752]{1,0:T(8,128)} %get-tuple-element.43) | copy-start | bytes 1032196
  125.1 6.2 %copy-start.15 = (f32[8,10752]{1,0:T(8,128)S(1)}, f32[8,10752]{1,0:T(8,128)}, u32[]{:S(2)}) copy-start(f32[8,10752]{1,0:T(8,128)} %get-tuple-element.21) | copy-start | bytes 1032196
  125.1 6.2 %copy-start.16 = (f32[8,10752]{1,0:T(8,128)S(1)}, f32[8,10752]{1,0:T(8,128)}, u32[]{:S(2)}) copy-start(f32[8,10752]{1,0:T(8,128)} %get-tuple-element.40) | copy-start | bytes 1032196
  125.1 6.0 %collective-permute-start.4 = (bf16[1,10752]{1,0:T(2,128)(2,1)S(1)}, bf16[1,10752]{1,0:T(2,128)(2,1)S(1)}, u32[]{:S(2)}, u32[]{:S(2)}) collective-permute-start(bf16[1,10752]{1,0:T(2,128)(2,1)S(1)} %slice.436), channel_id=1, source_target_pairs={{4,0},{8,4},{12,8},{16,12},{20,16},{24,20},{28,24},{5,1},{9,5},{13... | collective-permute-start | bytes 64520 | tf_op jit(solution)/shard_map/ppermute | solution.py:16
  131.6 4.9 %collective-permute-start.5 = (bf16[1,10752]{1,0:T(2,128)(2,1)S(1)}, bf16[1,10752]{1,0:T(2,128)(2,1)S(1)}, u32[]{:S(2)}, u32[]{:S(2)}) collective-permute-start(bf16[1,10752]{1,0:T(2,128)(2,1)S(1)} %slice.435), channel_id=1, source_target_pairs={{0,4},{4,8},{8,12},{12,16},{16,20},{20,24},{24,28},{1,5},{5,9},{9,... | collective-permute-start | bytes 64520 | tf_op jit(solution)/shard_map/ppermute | solution.py:16
  (20 other events, 34.8 us)
